TPU v7x, 512 devices: a whole 4x8x8 slice. The times are simulated.
512 devices in a mesh: dp: 32 (over y_lo, z, core), pipe: 16 (over x, y_hi).
Axes of the slice: x: 4, y: 8 (y_hi: 4, y_lo: 2; y = y_hi * 2 + y_lo), z: 8, core: 2. Of those that a mesh axis runs over, the one named last changes fastest.
Arguments:
- encoder_out: bfloat16 [2048, 8192], P('pipe', 'dp'), may hold values from -6 to 6
- key_value_weight: bfloat16 [16, 2048, 2048], P('pipe', 'dp'), may hold values from -0.125 to 0.125
- queries: bfloat16 [16, 8192, 1024], P('pipe', 'dp'), may hold values from -1.1953125 to 1.1953125
- context_gradient: bfloat16 [16, 8192, 1024], P('pipe', 'dp'), may hold values from -6 to 6
Outputs:
- context: bfloat16 [16, 8192, 1024], P('pipe', 'dp')
- grad_encoder: bfloat16 [2048, 8192], P('pipe', 'dp')
All inputs are finite; a program needn't handle non-finite values.
Results may differ from a plain program's by a relative error of at most 0.02.
Values may be sent and summed in bfloat16 or wider, within the bound.
A program may use at most 64 MiB of HBM per device.

v0:
```python
import jax
import jax.numpy as jnp
from jax import lax
from jax.sharding import PartitionSpec as P

LOCAL_HEADS = 8
HEAD_WIDTH = 128
ENCODER_LENGTH = 128
DECODER_LENGTH = 128


def attend(query_rows, grad_rows, key_value_rows, row_count, seq_len, dec_len, heads, head_size):
    width = heads * head_size
    key_rows = key_value_rows[:, :width].reshape(row_count, seq_len, heads, head_size)
    value_rows = key_value_rows[:, width:].reshape(row_count, seq_len, heads, head_size)
    query = query_rows.reshape(row_count, dec_len, heads, head_size)
    upstream = grad_rows.reshape(row_count, dec_len, heads, head_size)
    scores = jnp.einsum("bqhd,bkhd->bhqk", query, key_rows, preferred_element_type=jnp.float32)
    probs = jax.nn.softmax(scores, axis=-1)
    probs_bf = probs.astype(jnp.bfloat16)
    context = jnp.einsum(
        "bhqk,bkhd->bqhd", probs_bf, value_rows, preferred_element_type=jnp.float32
    ).astype(jnp.bfloat16)
    grad_probs = jnp.einsum(
        "bqhd,bkhd->bhqk", upstream, value_rows, preferred_element_type=jnp.float32
    )
    inner = jnp.sum(grad_probs * probs, axis=-1, keepdims=True)
    grad_scores = (probs * (grad_probs - inner)).astype(jnp.bfloat16)
    key_gradient = jnp.einsum(
        "bhqk,bqhd->bkhd", grad_scores, query, preferred_element_type=jnp.float32
    ).astype(jnp.bfloat16)
    value_gradient = jnp.einsum(
        "bhqk,bqhd->bkhd", probs_bf, upstream, preferred_element_type=jnp.float32
    ).astype(jnp.bfloat16)
    key_value_gradient = jnp.concatenate(
        [
            key_gradient.reshape(row_count * seq_len, width),
            value_gradient.reshape(row_count * seq_len, width),
        ],
        axis=1,
    )
    return (context.reshape(row_count * dec_len, width), key_value_gradient)


def local(encoder_out, key_value_weight, queries, context_gradient):
    local_weight = key_value_weight[0]
    tok_rows = encoder_out.shape[1]
    weights = lax.all_gather(local_weight, "dp", axis=0, tiled=True)
    rows = weights
    kv_sum = lax.dot_general(
        lax.all_gather(encoder_out, "pipe", axis=0, tiled=True),
        rows,
        (((0,), (0,)), ((), ())),
        preferred_element_type=jnp.float32,
    )
    key_value_rows = kv_sum.astype(jnp.bfloat16)
    row_count = tok_rows // ENCODER_LENGTH
    context, key_value_gradient = attend(
        queries[0],
        context_gradient[0],
        key_value_rows,
        row_count,
        ENCODER_LENGTH,
        DECODER_LENGTH,
        LOCAL_HEADS,
        HEAD_WIDTH,
    )
    rows = weights
    grad_encoder = lax.psum_scatter(
        lax.dot_general(
            rows, key_value_gradient, (((1,), (1,)), ((), ())), preferred_element_type=jnp.float32
        ).astype(jnp.bfloat16),
        "pipe",
        scatter_dimension=0,
        tiled=True,
    )
    return (context[None], grad_encoder)


def solution(mesh):
    return jax.shard_map(
        local,
        mesh=mesh,
        in_specs=(
            P("pipe", "dp"),
            P("pipe", "dp", None),
            P("pipe", "dp", None),
            P("pipe", "dp", None),
        ),
        out_specs=(P("pipe", "dp", None), P("pipe", "dp")),
        check_vma=False,
    )
```

profile of v0, /device:TPU:1, one launch (start us, length us, event | category | flops | bytes accessed | tf_op | source)
XLA Modules:
  0.0 260.4 jit_solution(7783968193602788068)
XLA Ops:
  7.2 0.0 all-gather.4.cloned.1.call-start
  7.2 0.7 all-gather.4.cloned.1.call-update
  7.9 0.0 all-gather.6.cloned.1.call-start
  7.9 0.7 all-gather.6.cloned.1.call-update
  8.6 0.0 reduce-scatter.4.cloned.1.call-start
  8.7 1.1 copy.44
  9.8 1.1 copy.45
  11.0 63.0 %all-gather.4.cloned.1.call-done = bf16[2048,256]{1,0:T(8,128)(2,1)} async-done(((bf16[128,256]{1,0:T(8,128)(2,1)}), bf16[2048,256]{1,0:T(8,128)(2,1)}) %all-gather.4.cloned.1.call-update) | async-done | bytes 1048592 | tf_op jit(solution)/shard_map/all_gather | solution.py:51
  74.0 76.6 %all-gather.6.cloned.1.call-done = bf16[1,2048,2048]{2,1,0:T(8,128)(2,1)} async-done(((bf16[1,64,2048]{2,1,0:T(8,128)(2,1)}), bf16[1,2048,2048]{2,1,0:T(8,128)(2,1)}) %all-gather.6.cloned.1.call-update) | async-done | bytes 8388624 | tf_op jit(solution)/shard_map/all_gather | solution.py:48
  150.5 6.1 %fusion.5 = bf16[256,2048]{1,0:T(8,128)(2,1)S(1)} fusion(bf16[2048,256]{1,0:T(8,128)(2,1)} %all-gather.4.cloned.1.call-done, bf16[1,2048,2048]{2,1,0:T(8,128)(2,1)} %all-gather.6.cloned.1.call-done), kind=kOutput, calls=%fused_computation.5 | convolution fusion | flops 2148007936 | bytes 10485760 | tf_op jit(solution)/shard_map/dot_general | solution.py:50
  156.6 0.1 slice_bitcast_fusion
  156.7 0.1 copy.43
  156.8 0.1 copy.42
  156.9 0.5 fusion.37
  157.4 0.0 slice-start
  157.5 0.3 fusion.18
  157.8 0.0 slice-start.1
  157.8 0.5 multiply_reduce_fusion
  158.3 0.4 fusion.17
  158.6 0.3 copy.35
  159.0 0.3 copy.37
  159.3 0.2 copy_bitcast_fusion
  159.5 0.1 slice-done
  159.6 1.4 slice-done.1
  161.0 2.4 fusion.11
  163.4 1.3 copy.40
  164.7 0.0 reduce-scatter.4.cloned.1.call-update
  164.7 0.3 fusion.16
  165.1 0.3 copy.31
  165.4 1.0 broadcast_in_dim_reshape.3
  166.4 87.5 %reduce-scatter.4.cloned.1.call-done = bf16[128,256]{1,0:T(8,128)(2,1)} async-done(((bf16[2048,256]{1,0:T(8,128)(2,1)}), bf16[128,256]{1,0:T(8,128)(2,1)}) %reduce-scatter.4.cloned.1.call-update) | async-done | bytes 65552
  (1 shorter events, 0.0 us)
Async XLA Ops:
  7.2 66.8 %all-gather.4.cloned.1.call-start = ((), (), s32[]{:S(2)}) async-start(), calls=%async_computation.1 | async-start | bytes 1114112 | tf_op jit(solution)/shard_map/all_gather | solution.py:51
  7.9 142.6 %all-gather.6.cloned.1.call-start = ((), (), s32[]{:S(2)}) async-start(), calls=%async_computation.2 | async-start | bytes 8650752 | tf_op jit(solution)/shard_map/all_gather | solution.py:48
  8.6 245.2 %reduce-scatter.4.cloned.1.call-start = ((), (), s32[]{:S(2)}) async-start(), calls=%async_computation.3 | async-start | bytes 1114112
  157.4 2.2 slice-start
  157.8 3.2 %slice-start.1 = ((s8[8388608]{0:T(1024)(128)(4,1)}), s8[4194304]{0:T(1024)(128)(4,1)S(1)}, s32[]{:S(2)}) async-start(s8[8388608]{0:T(1024)(128)(4,1)} %bitcast.55), calls=%async_computation.5 | async-start | bytes 8388608
Sparse Core Ops, SparseCore 0:
  11.0 62.8 all-gather.3
  76.1 74.3 all-gather.5
  164.8 88.9 reduce-scatter.3
where the time goes:
time: 261 us; the launch traced here: 260 us
  waiting for transfers between devices  228 us (87%)
  between operations  13.9 us (5%)
  matrix products  10.5 us (4%)
  local copies, waits for them, and re-layouts  7.51 us (3%)
    unnamed x4, waiting for transfers between devices  88.9 us
    all_gather x1, waiting for transfers between devices, local(): weights = lax.all_gather(local_weight, 'dp', axis=0, tiled=True)  76.6 us
    all_gather x1, waiting for transfers between devices, local(): lax.all_gather(encoder_out, 'pipe', axis=0, tiled=True)  63 us
    dot_general x1, matrix products, local(): lax.dot_general(lax.all_gather(encoder_out, 'pipe', axis=0, tiled=True),...  6.06 us
    unnamed x10, local copies, waits for them, and re-layouts  5.29 us
  transfers between devices with their start and end apart: 3, of which 3 were waited for; matrix products, arithmetic and copies ran while one was open for 2% of the time, Pallas kernels for 0%

commit v1 on v0

v1 whole, which is shorter than its diff:
```python
import jax
import jax.numpy as jnp
from jax import lax
from jax.experimental import pallas as pl
from jax.experimental.pallas import tpu as pltpu
from jax.sharding import PartitionSpec as P

MESH = pl.DeviceIdType.MESH
HEADS = 8
HD = 128
SEQ = 128
TOK = 256
WIDTH = 2048
NZ = 8
F32 = jnp.float32
BF16 = jnp.bfloat16


def nt(a, b):
    return lax.dot_general(a, b, (((1,), (1,)), ((), ())), preferred_element_type=F32)


def nn(a, b):
    return lax.dot_general(a, b, (((1,), (0,)), ((), ())), preferred_element_type=F32)


def kernel(
    enc_ref, w_ref, q_ref, cg_ref, ctx_ref, ge_ref,
    wb, w_st, enc_buf, enc_t, acc, q_v, cg_v, ctx_v, kv_v, gkv_v, xs, xr, ys, yr,
    loc, ring_s, ring_r, wy_s, wy_r, sib_s, sib_r, enc_s, enc_r, gx_s, gx_r, gy_s, gy_r,
):
    dp, pipe = lax.axis_index("dp"), lax.axis_index("pipe")
    core, z, row = dp % 2, (dp // 2) % NZ, dp // (2 * NZ)
    x, y = pipe // 4, pipe % 4
    dz = 1 - 2 * core
    orow = 1 - row

    def at_z(k):
        return (z + k * dz + 2 * NZ) % NZ

    def dp_of(r, zz, c):
        return {"dp": (r * NZ + zz) * 2 + c}

    def pipe_of(xx, yy):
        return {"pipe": xx * 4 + yy}

    far, near = dp_of(row, at_z(1), core), dp_of(row, at_z(-1), core)
    mate = dp_of(orow, z, core)
    twin = dp_of(row, z, 1 - core)
    xp, xm, xo = (x + 1) % 4, (x + 3) % 4, (x + 2) % 4
    yp, ym, yo = (y + 1) % 4, (y + 3) % 4, (y + 2) % 4
    x_up, x_dn = pipe_of(xp, y), pipe_of(xm, y)
    y_up, y_dn = pipe_of(x, yp), pipe_of(x, ym)

    started = []

    def send(src, dst, ss, rs, dev):
        c = pltpu.make_async_remote_copy(
            src_ref=src, dst_ref=dst, send_sem=ss, recv_sem=rs, device_id=dev, device_id_type=MESH
        )
        c.start()
        started.append(c)

    def arrived(dst, ss, rs, dev):
        pltpu.make_async_remote_copy(
            src_ref=dst, dst_ref=dst, send_sem=ss, recv_sem=rs, device_id=dev, device_id_type=MESH
        ).wait_recv()

    in_enc = pltpu.make_async_copy(enc_ref, enc_buf.at[:, pipe], loc.at[0])
    in_w = pltpu.make_async_copy(w_ref, w_st, loc.at[1])
    in_q = pltpu.make_async_copy(q_ref, q_v, loc.at[2])
    in_cg = pltpu.make_async_copy(cg_ref, cg_v, loc.at[3])
    in_enc.start()
    in_w.start()
    in_q.start()
    in_cg.start()

    barrier = pltpu.get_barrier_semaphore()
    for dev in (far, near, mate, twin, x_up, x_dn, y_up, y_dn):
        pl.semaphore_signal(barrier, inc=1, device_id=dev, device_id_type=MESH)
    pl.semaphore_wait(barrier, 8)

    groups = [("a", 0, 2), ("a", 2, 2), ("b", 4, 1), ("b", 5, 1), ("b", 6, 1), ("b", 7, 1)]

    def piece(g, zz):
        kind, h0, n = groups[g]
        if kind == "a":
            return wb.at[pl.ds(h0, n), core, row, zz]
        return wb.at[h0, core, :, zz]

    def rearrange(h):
        wb[h, core, row, z, :, :HD] = w_st[:, h * HD : (h + 1) * HD]
        wb[h, core, row, z, :, HD:] = w_st[:, (HEADS + h) * HD : (HEADS + h + 1) * HD]

    def mate_send(k, src):
        send(src, src, wy_s.at[k], wy_r.at[k], mate)

    def a_first(i, zz):
        s = wb.at[0, core, row, zz]
        mate_send(i, s)

    def ring(g, k):
        kind, h0, n = groups[g]
        if k >= 1:
            p = piece(g, at_z(-k))
            arrived(p, ring_s.at[g, k - 1], ring_r.at[g, k - 1], near)
            if k <= 3:
                p = piece(g, at_z(k))
                arrived(p, ring_s.at[g, 3 + k], ring_r.at[g, 3 + k], far)
        if k <= 3:
            p = piece(g, at_z(-k))
            send(p, p, ring_s.at[g, k], ring_r.at[g, k], far)
        if k <= 2:
            p = piece(g, at_z(k))
            send(p, p, ring_s.at[g, 4 + k], ring_r.at[g, 4 + k], near)
        if g == 0:
            a_first(k, at_z(-k))
            if 1 <= k <= 3:
                a_first(4 + k, at_z(k))
        if g == 5:
            p = piece(g, at_z(-k))
            send(p, p, sib_s.at[10 + k], sib_r.at[10 + k], twin)
            if 1 <= k <= 3:
                p = piece(g, at_z(k))
                send(p, p, sib_s.at[14 + k], sib_r.at[14 + k], twin)
        elif k == 4:
            if kind == "a":
                for h in range(max(h0, 1), h0 + n):
                    mate_send(7 + h, wb.at[h, core, row])
                p = wb.at[pl.ds(h0, n), core, row]
            else:
                p = wb.at[h0, core]
            send(p, p, sib_s.at[g], sib_r.at[g], twin)

    def mate_done(h):
        if h == 0:
            for i in range(8):
                zz = at_z(-i) if i <= 4 else at_z(i - 4)
                arrived(wb.at[0, core, orow, zz], wy_s.at[i], wy_r.at[i], mate)
        else:
            arrived(wb.at[h, core, orow], wy_s.at[7 + h], wy_r.at[7 + h], mate)
        p = wb.at[h, core, orow]
        send(p, p, sib_s.at[6 + h], sib_r.at[6 + h], twin)

    oc = 1 - core

    def twin_own(g):
        kind, h0, n = groups[g]
        if kind == "a":
            p = wb.at[pl.ds(h0, n), oc, row]
        else:
            p = wb.at[h0, oc]
        arrived(p, sib_s.at[g], sib_r.at[g], twin)

    def twin_done(h):
        if h < 4:
            arrived(wb.at[h, oc, orow], sib_s.at[6 + h], sib_r.at[6 + h], twin)
        elif h < 7:
            twin_own(h - 2)
        else:
            for k in range(5):
                arrived(wb.at[7, oc, :, (z + k * dz + 2 * NZ) % NZ], sib_s.at[10 + k], sib_r.at[10 + k], twin)
            for k in range(1, 4):
                arrived(wb.at[7, oc, :, at_z(-k)], sib_s.at[14 + k], sib_r.at[14 + k], twin)

    def enc_x(yy, i):
        b = enc_buf.at[:, x * 4 + yy]
        send(b, b, enc_s.at[4 + i], enc_r.at[4 + i], x_up)
        send(b, b, enc_s.at[8 + i], enc_r.at[8 + i], x_dn)

    def enc_x2(yy, i):
        b = enc_buf.at[:, xm * 4 + yy]
        arrived(b, enc_s.at[4 + i], enc_r.at[4 + i], x_dn)
        b = b.at[0]
        send(b, b, enc_s.at[12 + i], enc_r.at[12 + i], x_up)
        b = enc_buf.at[:, xp * 4 + yy]
        arrived(b, enc_s.at[8 + i], enc_r.at[8 + i], x_up)
        b = b.at[1]
        send(b, b, enc_s.at[16 + i], enc_r.at[16 + i], x_dn)

    def enc_0():
        b = enc_buf.at[:, pipe]
        send(b, b, enc_s.at[0], enc_r.at[0], y_up)
        send(b, b, enc_s.at[1], enc_r.at[1], y_dn)
        enc_x(y, 0)

    def enc_1():
        b = enc_buf.at[:, x * 4 + ym]
        arrived(b, enc_s.at[0], enc_r.at[0], y_dn)
        b = b.at[0]
        send(b, b, enc_s.at[2], enc_r.at[2], y_up)
        b = enc_buf.at[:, x * 4 + yp]
        arrived(b, enc_s.at[1], enc_r.at[1], y_up)
        b = b.at[1]
        send(b, b, enc_s.at[3], enc_r.at[3], y_dn)
        enc_x(ym, 1)
        enc_x(yp, 2)

    def enc_2():
        arrived(enc_buf.at[0, x * 4 + yo], enc_s.at[2], enc_r.at[2], y_dn)
        arrived(enc_buf.at[1, x * 4 + yo], enc_s.at[3], enc_r.at[3], y_up)
        enc_x(yo, 3)

    def enc_end():
        for i, yy in enumerate((y, ym, yp, yo)):
            arrived(enc_buf.at[0, xo * 4 + yy], enc_s.at[12 + i], enc_r.at[12 + i], x_dn)
            arrived(enc_buf.at[1, xo * 4 + yy], enc_s.at[16 + i], enc_r.at[16 + i], x_up)

    def transpose(c):
        b = enc_buf[c // 2, (c % 2) * 8 : (c % 2) * 8 + 8]
        enc_t[:, c * 512 : (c + 1) * 512] = b.reshape(512, TOK).T

    def project(h):
        w = wb[h].reshape(WIDTH, 2 * HD)
        kv_v[...] = nn(enc_t[...], w).astype(BF16)

    def attend(h, i):
        rows = slice(i * SEQ, (i + 1) * SEQ)
        cols = slice(h * HD, (h + 1) * HD)
        k, v = kv_v[rows, :HD], kv_v[rows, HD:]
        q, cg = q_v[rows, cols], cg_v[rows, cols]
        s = nt(k, q)
        e = jnp.exp(s - jnp.max(s, axis=0, keepdims=True))
        p = e / jnp.sum(e, axis=0, keepdims=True)
        pb = p.astype(BF16)
        ctx_v[rows, cols] = nn(pb.T, v).astype(BF16)
        gp = nt(v, cg)
        inner = jnp.sum(gp * p, axis=0, keepdims=True)
        gs = (p * (gp - inner)).astype(BF16)
        gkv_v[rows, :HD] = nn(gs, q).astype(BF16)
        gkv_v[rows, HD:] = nn(pb, cg).astype(BF16)

    def grad(h):
        g = gkv_v[...]
        for c in range(4):
            j, r = c // 2, c % 2
            t = nt(wb[h, j, r].reshape(512, 2 * HD), g).reshape(NZ, 64, TOK)
            acc[j, r] = t if first[0] else acc[j, r] + t
        first[0] = False

    first = [True]

    def head(h, during=()):
        twin_done(h)
        project(h)
        for f in during[:1]:
            f()
        attend(h, 0)
        attend(h, 1)
        for f in during[1:2]:
            f()
        grad(h)
        for f in during[2:]:
            f()

    in_enc.wait()
    enc_0()
    in_w.wait()
    rearrange(0)
    rearrange(1)
    ring(0, 0)
    rearrange(2)
    rearrange(3)
    ring(1, 0)
    for h in range(4, 8):
        rearrange(h)
    p = wb.at[pl.ds(4, 4), core, row, z]
    mate_send(11, p)
    enc_1()
    ring(0, 1)
    enc_x2(y, 0)
    ring(1, 1)
    enc_2()
    ring(0, 2)
    enc_x2(ym, 1)
    enc_x2(yp, 2)
    ring(1, 2)
    arrived(wb.at[pl.ds(4, 4), core, orow, z], wy_s.at[11], wy_r.at[11], mate)
    ring(2, 0)
    ring(0, 3)
    enc_x2(yo, 3)
    ring(1, 3)
    ring(2, 1)
    ring(0, 4)
    ring(3, 0)
    ring(1, 4)
    enc_end()
    in_q.wait()
    in_cg.wait()
    transpose(0)
    transpose(1)
    ring(2, 2)
    transpose(2)
    transpose(3)
    ring(3, 1)
    mate_done(0)
    ring(2, 3)
    twin_own(0)
    head(0, (lambda: ring(3, 2), lambda: ring(4, 0), lambda: ring(2, 4)))
    ring(3, 3)
    ring(4, 1)
    mate_done(1)
    head(4, (lambda: ring(3, 4), lambda: ring(4, 2), lambda: ring(5, 0)))
    ring(4, 3)
    ring(5, 1)
    head(1, (lambda: ring(4, 4), lambda: mate_done(2), lambda: ring(5, 2)))
    head(5, (lambda: ring(5, 3),))
    twin_own(1)
    head(2)
    ring(5, 4)
    head(6)
    mate_done(3)
    head(3)

    twin_done(7)
    project(7)
    attend(7, 0)
    attend(7, 1)
    out_ctx = pltpu.make_async_copy(ctx_v, ctx_ref, loc.at[4])
    out_ctx.start()
    g7 = gkv_v[...]
    order = (yo, yp, ym, y)

    def blocks(ref, j, xx):
        return ref.at[j, xx // 2, pl.ds((xx % 2) * 4, 4)]

    def last(j, xx):
        w = blocks(wb.at[7], j, xx)[...].reshape(TOK, 2 * HD)
        return blocks(acc, j, xx)[...] + nt(w, g7).reshape(4, 64, TOK)

    def one(j, xx, yy):
        return acc.at[j, xx // 2, (xx % 2) * 4 + yy]

    def gx(m, r):
        send(xs.at[m, order[r]], xr.at[m, order[r]], gx_s.at[m, r], gx_r.at[m, r], x_up if m % 2 == 0 else x_dn)

    def gx_in(m, r):
        dev = x_dn if m % 2 == 0 else x_up
        arrived(xr.at[m, order[r]], gx_s.at[m, r], gx_r.at[m, r], dev)
        return xr[m, order[r]].astype(F32)

    for m, (j, xx) in enumerate(((0, xo), (1, xo), (1, xp), (0, xm))):
        xs[m] = last(j, xx).astype(BF16)
        if m in (1, 3):
            for r in range(4):
                gx(m - 1, r)
                gx(m, r)
    for j, xx in ((0, xp), (1, xm), (0, x), (1, x)):
        blocks(acc, j, xx)[...] = last(j, xx)
    for r in range(4):
        xs[4, order[r]] = (gx_in(0, r) + one(0, xp, order[r])[...]).astype(BF16)
        gx(4, r)
        xs[5, order[r]] = (gx_in(1, r) + one(1, xm, order[r])[...]).astype(BF16)
        gx(5, r)

    def total(r):
        t1 = one(1, x, order[r])[...] + gx_in(2, r)
        t0 = one(0, x, order[r])[...] + gx_in(3, r)
        return t0 + gx_in(4, r), t1 + gx_in(5, r)

    def gy(m, v):
        ys[m] = v.astype(BF16)
        send(ys.at[m], yr.at[m], gy_s.at[m], gy_r.at[m], y_up if m % 2 == 0 else y_dn)

    def gy_in(m):
        arrived(yr.at[m], gy_s.at[m], gy_r.at[m], y_dn if m % 2 == 0 else y_up)
        return yr[m].astype(F32)

    s0, s1 = total(0)
    gy(0, s0)
    gy(1, s1)
    u0, u1 = total(1)
    gy(2, u1)
    gy(4, u0 + gy_in(0))
    d0, d1 = total(2)
    gy(3, d0)
    gy(5, d1 + gy_in(1))
    o0, o1 = total(3)
    ge_ref[0] = (o0 + gy_in(3) + gy_in(4)).astype(BF16)
    ge_ref[1] = (o1 + gy_in(2) + gy_in(5)).astype(BF16)

    for c in started:
        c.wait_send()
    out_ctx.wait()


def local(encoder_out, key_value_weight, queries, context_gradient):
    any_space = pl.BlockSpec(memory_space=pl.ANY)
    vmem = pl.BlockSpec(memory_space=pltpu.VMEM)
    dma = pltpu.SemaphoreType.DMA
    ctx, ge = pl.pallas_call(
        kernel,
        out_shape=(
            jax.ShapeDtypeStruct((TOK, HEADS * HD), BF16),
            jax.ShapeDtypeStruct((2, 64, TOK), BF16),
        ),
        in_specs=[any_space] * 4,
        out_specs=(any_space, vmem),
        scratch_shapes=[
            pltpu.VMEM((HEADS, 2, 2, NZ, 64, 2 * HD), BF16),
            pltpu.VMEM((64, WIDTH), BF16),
            pltpu.VMEM((2, 16, 64, TOK), BF16),
            pltpu.VMEM((TOK, WIDTH), BF16),
            pltpu.VMEM((2, 2, NZ, 64, TOK), F32),
            pltpu.VMEM((TOK, HEADS * HD), BF16),
            pltpu.VMEM((TOK, HEADS * HD), BF16),
            pltpu.VMEM((TOK, HEADS * HD), BF16),
            pltpu.VMEM((TOK, 2 * HD), BF16),
            pltpu.VMEM((TOK, 2 * HD), BF16),
            pltpu.VMEM((6, 4, 64, TOK), BF16),
            pltpu.VMEM((6, 4, 64, TOK), BF16),
            pltpu.VMEM((6, 64, TOK), BF16),
            pltpu.VMEM((6, 64, TOK), BF16),
            dma((5,)),
            dma((6, 7)),
            dma((6, 7)),
            dma((12,)),
            dma((12,)),
            dma((18,)),
            dma((18,)),
            dma((20,)),
            dma((20,)),
            dma((6, 4)),
            dma((6, 4)),
            dma((6,)),
            dma((6,)),
        ],
        compiler_params=pltpu.CompilerParams(
            collective_id=0, has_side_effects=True, vmem_limit_bytes=48 * 1024 * 1024
        ),
    )(
        encoder_out.reshape(2, 64, TOK),
        key_value_weight[0],
        queries[0],
        context_gradient[0],
    )
    return ctx[None], ge.reshape(2 * 64, TOK)


def solution(mesh):
    return jax.shard_map(
        local,
        mesh=mesh,
        in_specs=(P("pipe", "dp"), P("pipe", "dp", None), P("pipe", "dp", None), P("pipe", "dp", None)),
        out_specs=(P("pipe", "dp", None), P("pipe", "dp")),
        check_vma=False,
    )
```

time: 261 us -> 102 us (0.39)
  waiting for transfers between devices: 228 us -> 0 us
  Pallas kernels: 0 us -> 95.4 us
  between operations: 13.9 us -> 0.65 us
  matrix products: 10.5 us -> 0 us
    all_gather x2 -> x0, waiting for transfers between devices: 140 us -> none  [the longest x1 76.6 us: local(): weights = lax.all_gather(local_weight, 'dp', axis=0, tiled=True)]
    pallas_call x0 -> x1, Pallas kernels: none -> 95.4 us  [local(): pl.pallas_call(kernel, out_shape=(jax.ShapeDtypeStruct((TOK, HEADS * HD),...]
    unnamed x4 -> x0, waiting for transfers between devices: 88.9 us -> none
    dot_general x6 -> x0, matrix products: 9.92 us -> none  [the longest x1 6.06 us: local(): lax.dot_general(lax.all_gather(encoder_out, 'pipe', axis=0, tiled=True),...]
  transfers between devices with their start and end apart: 3 -> 0, of which waited for: 3 -> 0; matrix products, arithmetic and copies ran while one was open for 2% -> 0% of each run, Pallas kernels for 0% -> 0%
where the time goes in v1:
time: 102 us; the launch traced here: 101 us
  Pallas kernels  95.4 us (94%)
  local copies, waits for them, and re-layouts  5.29 us (5%)
    pallas_call x1, Pallas kernels, local(): pl.pallas_call(kernel, out_shape=(jax.ShapeDtypeStruct((TOK, HEADS * HD),...  95.4 us
    unnamed x10, local copies, waits for them, and re-layouts  5.29 us

profile of v1, /device:TPU:1, one launch (start us, length us, event | category | flops | bytes accessed | tf_op | source)
XLA Modules:
  0.0 101.3 jit_solution(11328275967409778168)
XLA Ops:
  0.6 0.0 copy-start
  0.6 1.0 %copy-done = bf16[1,256,1024]{2,1,0:T(8,128)(2,1)S(1)} copy-done((bf16[1,256,1024]{2,1,0:T(8,128)(2,1)S(1)}, bf16[1,256,1024]{2,1,0:T(8,128)(2,1)}, u32[]{:S(2)}) %copy-start) | copy-done | bytes 524312
  1.7 0.0 copy-start.1
  1.7 1.0 %copy-done.1 = bf16[1,256,1024]{2,1,0:T(8,128)(2,1)S(1)} copy-done((bf16[1,256,1024]{2,1,0:T(8,128)(2,1)S(1)}, bf16[1,256,1024]{2,1,0:T(8,128)(2,1)}, u32[]{:S(2)}) %copy-start.1) | copy-done | bytes 524312
  2.7 0.0 copy-start.2
  2.7 0.9 copy-done.2
  3.7 0.0 copy-start.3
  3.7 0.8 copy-done.3
  4.5 95.4 %shard_map.59 = (bf16[256,1024]{1,0:T(8,128)(2,1)S(1)}, bf16[2,64,256]{2,1,0:T(8,128)(2,1)S(1)}) custom-call(bf16[2,64,256]{2,1,0:T(8,128)(2,1)S(1)} %bitcast.11, bf16[64,2048]{1,0:T(8,128)(2,1)S(1)} %bitcast.9, bf16[256,1024]{1,0:T(8,128)(2,1)S(1)} %bitcast.6, bf16[256,1024]{1,0:T(8,128)(2,1)S(1)} %bitcast.7), custom_call_target="tpu_custom_call" | custom-call | tf_op jit(solution)/shard_map/pallas_call | solution.py:391
  99.9 0.8 copy.8
  100.7 0.6 copy.9
Async XLA Ops:
  0.6 1.0 %copy-start = (bf16[1,256,1024]{2,1,0:T(8,128)(2,1)S(1)}, bf16[1,256,1024]{2,1,0:T(8,128)(2,1)}, u32[]{:S(2)}) copy-start(bf16[1,256,1024]{2,1,0:T(8,128)(2,1)} %param.6) | copy-start | bytes 1572868
  1.7 1.0 %copy-start.1 = (bf16[1,256,1024]{2,1,0:T(8,128)(2,1)S(1)}, bf16[1,256,1024]{2,1,0:T(8,128)(2,1)}, u32[]{:S(2)}) copy-start(bf16[1,256,1024]{2,1,0:T(8,128)(2,1)} %param.7) | copy-start | bytes 1572868
  2.7 0.9 copy-start.2
  3.7 0.8 copy-start.3

commit v2 on v1

--- a/solution.py
+++ b/solution.py
@@ -12,9 +12,25 @@
 TOK = 256
 WIDTH = 2048
 NZ = 8
+LIMIT = 62
 F32 = jnp.float32
 BF16 = jnp.bfloat16
 
+ORDER = [
+    ("e0",), ("yb",), ("F", 0, 0), ("N", 0, 0), ("F", 1, 0), ("N", 1, 0), ("F", 0, 1), ("ex", 0), ("N", 0, 1),
+    ("F", 1, 1), ("N", 1, 1), ("e1",), ("F", 0, 2), ("N", 0, 2), ("F", 1, 2), ("ybw",), ("F", 2, 0),
+    ("N", 2, 0), ("N", 1, 2), ("ex", 1), ("F", 0, 3), ("N", 0, 3), ("F", 3, 0), ("N", 3, 0), ("ex", 2),
+    ("F", 1, 3), ("F", 2, 1), ("N", 2, 1), ("e2",), ("N", 1, 3), ("F", 0, 4), ("F", 4, 0), ("N", 4, 0),
+    ("end", 0), ("ys", 1), ("F", 3, 1), ("N", 3, 1), ("ex", 3), ("F", 1, 4), ("end", 1), ("ys", 2), ("yd", 0),
+    ("ys", 3), ("F", 2, 2), ("N", 2, 2), ("F", 4, 1), ("ee",), ("t", 0), ("N", 4, 1), ("t", 1), ("t", 2),
+    ("t", 3), ("F", 3, 2), ("P", 0), ("A", 0), ("N", 3, 2), ("G", 0), ("F", 2, 3), ("N", 2, 3), ("F", 5, 0),
+    ("N", 5, 0), ("yd", 1), ("F", 4, 2), ("N", 4, 2), ("F", 3, 3), ("P", 1), ("A", 1), ("N", 3, 3), ("G", 1),
+    ("F", 2, 4), ("end", 2), ("F", 5, 1), ("N", 5, 1), ("F", 4, 3), ("P", 4), ("yd", 2), ("N", 4, 3),
+    ("A", 4), ("F", 3, 4), ("end", 3), ("G", 4), ("F", 5, 2), ("P", 2), ("A", 2), ("N", 5, 2), ("G", 2),
+    ("F", 4, 4), ("end", 4), ("P", 5), ("A", 5), ("F", 5, 3), ("G", 5), ("N", 5, 3), ("P", 6), ("yd", 3),
+    ("A", 6), ("G", 6), ("F", 5, 4), ("end", 5), ("P", 3), ("A", 3), ("G", 3), ("P", 7), ("A", 7),
+]
+
 
 def nt(a, b):
     return lax.dot_general(a, b, (((1,), (1,)), ((), ())), preferred_element_type=F32)
@@ -22,6 +38,10 @@
 
 def nn(a, b):
     return lax.dot_general(a, b, (((1,), (0,)), ((), ())), preferred_element_type=F32)
+
+
+def tn(a, b):
+    return lax.dot_general(a, b, (((0,), (0,)), ((), ())), preferred_element_type=F32)
 
 
 def kernel(
@@ -95,42 +115,49 @@
     def mate_send(k, src):
         send(src, src, wy_s.at[k], wy_r.at[k], mate)
 
-    def a_first(i, zz):
-        s = wb.at[0, core, row, zz]
-        mate_send(i, s)
-
-    def ring(g, k):
+    def spread(g, k, zz):
+        if g == 0:
+            mate_send(k, wb.at[0, core, row, zz])
+        if g == 5:
+            p = piece(g, zz)
+            send(p, p, sib_s.at[10 + k], sib_r.at[10 + k], twin)
+
+    def far_step(g, k):
+        p = piece(g, at_z(-k))
+        if k >= 1:
+            arrived(p, ring_s.at[g, k - 1], ring_r.at[g, k - 1], near)
+        elif g < 2:
+            for h in range(2 * g, 2 * g + 2):
+                rearrange(h)
+        if k <= 3:
+            send(p, p, ring_s.at[g, k], ring_r.at[g, k], far)
+        spread(g, k, at_z(-k))
+
+    def near_step(g, k):
+        p = piece(g, at_z(k))
+        if k >= 1:
+            arrived(p, ring_s.at[g, 3 + k], ring_r.at[g, 3 + k], far)
+        if k <= 2:
+            send(p, p, ring_s.at[g, 4 + k], ring_r.at[g, 4 + k], near)
+        if k >= 1:
+            spread(g, 4 + k, at_z(k))
+
+    def group_end(g):
         kind, h0, n = groups[g]
-        if k >= 1:
-            p = piece(g, at_z(-k))
-            arrived(p, ring_s.at[g, k - 1], ring_r.at[g, k - 1], near)
-            if k <= 3:
-                p = piece(g, at_z(k))
-                arrived(p, ring_s.at[g, 3 + k], ring_r.at[g, 3 + k], far)
-        if k <= 3:
-            p = piece(g, at_z(-k))
-            send(p, p, ring_s.at[g, k], ring_r.at[g, k], far)
-        if k <= 2:
-            p = piece(g, at_z(k))
-            send(p, p, ring_s.at[g, 4 + k], ring_r.at[g, 4 + k], near)
-        if g == 0:
-            a_first(k, at_z(-k))
-            if 1 <= k <= 3:
-                a_first(4 + k, at_z(k))
-        if g == 5:
-            p = piece(g, at_z(-k))
-            send(p, p, sib_s.at[10 + k], sib_r.at[10 + k], twin)
-            if 1 <= k <= 3:
-                p = piece(g, at_z(k))
-                send(p, p, sib_s.at[14 + k], sib_r.at[14 + k], twin)
-        elif k == 4:
-            if kind == "a":
-                for h in range(max(h0, 1), h0 + n):
-                    mate_send(7 + h, wb.at[h, core, row])
-                p = wb.at[pl.ds(h0, n), core, row]
-            else:
-                p = wb.at[h0, core]
+        if g < 5:
+            p = wb.at[pl.ds(h0, n), core, row] if kind == "a" else wb.at[h0, core]
             send(p, p, sib_s.at[g], sib_r.at[g], twin)
+
+    def mate_bulk(h):
+        mate_send(7 + h, wb.at[h, core, row])
+
+    def mate_b():
+        for h in range(4, 8):
+            rearrange(h)
+        mate_send(11, wb.at[pl.ds(4, 4), core, row, z])
+
+    def mate_b_in():
+        arrived(wb.at[pl.ds(4, 4), core, orow, z], wy_s.at[11], wy_r.at[11], mate)
 
     def mate_done(h):
         if h == 0:
@@ -158,10 +185,9 @@
         elif h < 7:
             twin_own(h - 2)
         else:
-            for k in range(5):
-                arrived(wb.at[7, oc, :, (z + k * dz + 2 * NZ) % NZ], sib_s.at[10 + k], sib_r.at[10 + k], twin)
-            for k in range(1, 4):
-                arrived(wb.at[7, oc, :, at_z(-k)], sib_s.at[14 + k], sib_r.at[14 + k], twin)
+            for k in range(8):
+                zz = at_z(k) if k <= 4 else at_z(4 - k)
+                arrived(wb.at[7, oc, :, zz], sib_s.at[10 + k], sib_r.at[10 + k], twin)
 
     def enc_x(yy, i):
         b = enc_buf.at[:, x * 4 + yy]
@@ -214,21 +240,24 @@
         w = wb[h].reshape(WIDTH, 2 * HD)
         kv_v[...] = nn(enc_t[...], w).astype(BF16)
 
-    def attend(h, i):
-        rows = slice(i * SEQ, (i + 1) * SEQ)
+    def attend(h):
         cols = slice(h * HD, (h + 1) * HD)
-        k, v = kv_v[rows, :HD], kv_v[rows, HD:]
-        q, cg = q_v[rows, cols], cg_v[rows, cols]
-        s = nt(k, q)
-        e = jnp.exp(s - jnp.max(s, axis=0, keepdims=True))
-        p = e / jnp.sum(e, axis=0, keepdims=True)
-        pb = p.astype(BF16)
-        ctx_v[rows, cols] = nn(pb.T, v).astype(BF16)
-        gp = nt(v, cg)
-        inner = jnp.sum(gp * p, axis=0, keepdims=True)
-        gs = (p * (gp - inner)).astype(BF16)
-        gkv_v[rows, :HD] = nn(gs, q).astype(BF16)
-        gkv_v[rows, HD:] = nn(pb, cg).astype(BF16)
+        rows = [slice(i * SEQ, (i + 1) * SEQ) for i in range(TOK // SEQ)]
+        k = [kv_v[r, :HD] for r in rows]
+        v = [kv_v[r, HD:] for r in rows]
+        q = [q_v[r, cols] for r in rows]
+        cg = [cg_v[r, cols] for r in rows]
+        s = [nt(a, b) for a, b in zip(k, q)]
+        gp = [nt(a, b) for a, b in zip(v, cg)]
+        e = [jnp.exp(t - jnp.max(t, axis=0, keepdims=True)) for t in s]
+        p = [t * (1.0 / jnp.sum(t, axis=0, keepdims=True)) for t in e]
+        pb = [t.astype(BF16) for t in p]
+        gs = [(a * (b - jnp.sum(b * a, axis=0, keepdims=True))).astype(BF16) for a, b in zip(p, gp)]
+        for i, r in enumerate(rows):
+            gkv_v[r, :HD] = nn(gs[i], q[i]).astype(BF16)
+            gkv_v[r, HD:] = nn(pb[i], cg[i]).astype(BF16)
+        for i, r in enumerate(rows):
+            ctx_v[r, cols] = tn(pb[i], v[i]).astype(BF16)
 
     def grad(h):
         g = gkv_v[...]
@@ -240,82 +269,36 @@
 
     first = [True]
 
-    def head(h, during=()):
+    def own_start():
+        in_enc.wait()
+        enc_0()
+        in_w.wait()
+
+    def enc_hop(i):
+        enc_x2((y, ym, yp, yo)[i], i)
+
+    def enc_all():
+        enc_end()
+        in_q.wait()
+        in_cg.wait()
+
+    owned = set()
+
+    def project_step(h):
+        if h < 4 and h // 2 not in owned:
+            owned.add(h // 2)
+            twin_own(h // 2)
         twin_done(h)
         project(h)
-        for f in during[:1]:
-            f()
-        attend(h, 0)
-        attend(h, 1)
-        for f in during[1:2]:
-            f()
-        grad(h)
-        for f in during[2:]:
-            f()
-
-    in_enc.wait()
-    enc_0()
-    in_w.wait()
-    rearrange(0)
-    rearrange(1)
-    ring(0, 0)
-    rearrange(2)
-    rearrange(3)
-    ring(1, 0)
-    for h in range(4, 8):
-        rearrange(h)
-    p = wb.at[pl.ds(4, 4), core, row, z]
-    mate_send(11, p)
-    enc_1()
-    ring(0, 1)
-    enc_x2(y, 0)
-    ring(1, 1)
-    enc_2()
-    ring(0, 2)
-    enc_x2(ym, 1)
-    enc_x2(yp, 2)
-    ring(1, 2)
-    arrived(wb.at[pl.ds(4, 4), core, orow, z], wy_s.at[11], wy_r.at[11], mate)
-    ring(2, 0)
-    ring(0, 3)
-    enc_x2(yo, 3)
-    ring(1, 3)
-    ring(2, 1)
-    ring(0, 4)
-    ring(3, 0)
-    ring(1, 4)
-    enc_end()
-    in_q.wait()
-    in_cg.wait()
-    transpose(0)
-    transpose(1)
-    ring(2, 2)
-    transpose(2)
-    transpose(3)
-    ring(3, 1)
-    mate_done(0)
-    ring(2, 3)
-    twin_own(0)
-    head(0, (lambda: ring(3, 2), lambda: ring(4, 0), lambda: ring(2, 4)))
-    ring(3, 3)
-    ring(4, 1)
-    mate_done(1)
-    head(4, (lambda: ring(3, 4), lambda: ring(4, 2), lambda: ring(5, 0)))
-    ring(4, 3)
-    ring(5, 1)
-    head(1, (lambda: ring(4, 4), lambda: mate_done(2), lambda: ring(5, 2)))
-    head(5, (lambda: ring(5, 3),))
-    twin_own(1)
-    head(2)
-    ring(5, 4)
-    head(6)
-    mate_done(3)
-    head(3)
-
-    twin_done(7)
-    project(7)
-    attend(7, 0)
-    attend(7, 1)
+
+    steps = {
+        "e0": own_start, "e1": enc_1, "e2": enc_2, "ex": enc_hop, "ee": enc_all, "t": transpose,
+        "yb": mate_b, "ybw": mate_b_in, "F": far_step, "N": near_step, "end": group_end,
+        "ys": mate_bulk, "yd": mate_done, "P": project_step, "A": attend, "G": grad,
+    }
+    for name, *at in ORDER:
+        steps[name](*at)
+
     out_ctx = pltpu.make_async_copy(ctx_v, ctx_ref, loc.at[4])
     out_ctx.start()
     g7 = gkv_v[...]
@@ -339,20 +322,36 @@
         arrived(xr.at[m, order[r]], gx_s.at[m, r], gx_r.at[m, r], dev)
         return xr[m, order[r]].astype(F32)
 
-    for m, (j, xx) in enumerate(((0, xo), (1, xo), (1, xp), (0, xm))):
-        xs[m] = last(j, xx).astype(BF16)
-        if m in (1, 3):
-            for r in range(4):
-                gx(m - 1, r)
-                gx(m, r)
-    for j, xx in ((0, xp), (1, xm), (0, x), (1, x)):
-        blocks(acc, j, xx)[...] = last(j, xx)
-    for r in range(4):
+    def relay(r):
         xs[4, order[r]] = (gx_in(0, r) + one(0, xp, order[r])[...]).astype(BF16)
         gx(4, r)
         xs[5, order[r]] = (gx_in(1, r) + one(1, xm, order[r])[...]).astype(BF16)
         gx(5, r)
 
+    def pair(m, r):
+        gx(m, r)
+        gx(m + 1, r)
+
+    xs[0] = last(0, xo).astype(BF16)
+    xs[1] = last(1, xo).astype(BF16)
+    pair(0, 0)
+    pair(0, 1)
+    xs[2] = last(1, xp).astype(BF16)
+    xs[3] = last(0, xm).astype(BF16)
+    pair(2, 0)
+    pair(0, 2)
+    blocks(acc, 0, xp)[...] = last(0, xp)
+    blocks(acc, 1, xm)[...] = last(1, xm)
+    relay(0)
+    pair(0, 3)
+    pair(2, 1)
+    blocks(acc, 0, x)[...] = last(0, x)
+    blocks(acc, 1, x)[...] = last(1, x)
+    relay(1)
+    pair(2, 2)
+    relay(2)
+    pair(2, 3)
+
     def total(r):
         t1 = one(1, x, order[r])[...] + gx_in(2, r)
         t0 = one(0, x, order[r])[...] + gx_in(3, r)
@@ -369,11 +368,12 @@
     s0, s1 = total(0)
     gy(0, s0)
     gy(1, s1)
+    relay(3)
     u0, u1 = total(1)
     gy(2, u1)
-    gy(4, u0 + gy_in(0))
     d0, d1 = total(2)
     gy(3, d0)
+    gy(4, u0 + gy_in(0))
     gy(5, d1 + gy_in(1))
     o0, o1 = total(3)
     ge_ref[0] = (o0 + gy_in(3) + gy_in(4)).astype(BF16)
@@ -426,7 +426,7 @@
             dma((6,)),
         ],
         compiler_params=pltpu.CompilerParams(
-            collective_id=0, has_side_effects=True, vmem_limit_bytes=48 * 1024 * 1024
+            collective_id=0, has_side_effects=True, vmem_limit_bytes=LIMIT * 1024 * 1024
         ),
     )(
         encoder_out.reshape(2, 64, TOK),

time: 102 us -> 76.5 us (0.75)
  Pallas kernels: 95.4 us -> 72 us
  local copies, waits for them, and re-layouts: 5.29 us -> 2.53 us
    pallas_call x1, Pallas kernels: 95.4 us -> 72 us  [local(): pl.pallas_call(kernel, out_shape=(jax.ShapeDtypeStruct((TOK, HEADS * HD),...]
    unnamed x10 -> x4, local copies, waits for them, and re-layouts: 5.29 us -> 2.53 us
where the time goes in v2:
time: 76.5 us; the launch traced here: 75.2 us
  Pallas kernels  72 us (94%)
  local copies, waits for them, and re-layouts  2.53 us (3%)
    pallas_call x1, Pallas kernels, local(): pl.pallas_call(kernel, out_shape=(jax.ShapeDtypeStruct((TOK, HEADS * HD),...  72 us
    unnamed x4, local copies, waits for them, and re-layouts  2.53 us

profile of v2, /device:TPU:1, one launch (start us, length us, event | category | flops | bytes accessed | tf_op | source)
XLA Modules:
  0.0 75.2 jit_solution(12892764908360902171)
XLA Ops:
  0.6 72.0 %shard_map.59 = (bf16[256,1024]{1,0:T(8,128)(2,1)}, bf16[2,64,256]{2,1,0:T(8,128)(2,1)}) custom-call(bf16[2,64,256]{2,1,0:T(8,128)(2,1)} %bitcast.11, bf16[64,2048]{1,0:T(8,128)(2,1)} %bitcast.9, bf16[256,1024]{1,0:T(8,128)(2,1)} %bitcast.6, bf16[256,1024]{1,0:T(8,128)(2,1)} %bitcast.7), custom_call_target="tpu_custom_call" | custom-call | tf_op jit(solution)/shard_map/pallas_call | solution.py:391
  72.7 0.0 copy-start
  72.7 1.9 %copy.8 = bf16[1,256,1024]{2,1,0:T(8,128)(2,1)} copy(bf16[1,256,1024]{2,1,0:T(8,128)(2,1)} %bitcast.8) | data formatting | bytes 1048576
  74.6 0.0 copy-done
  74.6 0.6 copy.9
Async XLA Ops:
  72.7 1.9 %copy-start = (bf16[2,64,256]{2,1,0:T(8,128)(2,1)S(1)}, bf16[2,64,256]{2,1,0:T(8,128)(2,1)}, u32[]{:S(2)}) copy-start(bf16[2,64,256]{2,1,0:T(8,128)(2,1)} %get-tuple-element.5) | copy-start | bytes 196612

commit v3 on v2

--- a/solution.py
+++ b/solution.py
@@ -12,23 +12,24 @@
 TOK = 256
 WIDTH = 2048
 NZ = 8
-LIMIT = 62
+PARTS = 4
+LIMIT = 63488
 F32 = jnp.float32
 BF16 = jnp.bfloat16
 
 ORDER = [
     ("e0",), ("yb",), ("F", 0, 0), ("N", 0, 0), ("F", 1, 0), ("N", 1, 0), ("F", 0, 1), ("ex", 0), ("N", 0, 1),
     ("F", 1, 1), ("N", 1, 1), ("e1",), ("F", 0, 2), ("N", 0, 2), ("F", 1, 2), ("ybw",), ("F", 2, 0),
-    ("N", 2, 0), ("N", 1, 2), ("ex", 1), ("F", 0, 3), ("N", 0, 3), ("F", 3, 0), ("N", 3, 0), ("ex", 2),
-    ("F", 1, 3), ("F", 2, 1), ("N", 2, 1), ("e2",), ("N", 1, 3), ("F", 0, 4), ("F", 4, 0), ("N", 4, 0),
-    ("end", 0), ("ys", 1), ("F", 3, 1), ("N", 3, 1), ("ex", 3), ("F", 1, 4), ("end", 1), ("ys", 2), ("yd", 0),
-    ("ys", 3), ("F", 2, 2), ("N", 2, 2), ("F", 4, 1), ("ee",), ("t", 0), ("N", 4, 1), ("t", 1), ("t", 2),
-    ("t", 3), ("F", 3, 2), ("P", 0), ("A", 0), ("N", 3, 2), ("G", 0), ("F", 2, 3), ("N", 2, 3), ("F", 5, 0),
-    ("N", 5, 0), ("yd", 1), ("F", 4, 2), ("N", 4, 2), ("F", 3, 3), ("P", 1), ("A", 1), ("N", 3, 3), ("G", 1),
-    ("F", 2, 4), ("end", 2), ("F", 5, 1), ("N", 5, 1), ("F", 4, 3), ("P", 4), ("yd", 2), ("N", 4, 3),
-    ("A", 4), ("F", 3, 4), ("end", 3), ("G", 4), ("F", 5, 2), ("P", 2), ("A", 2), ("N", 5, 2), ("G", 2),
-    ("F", 4, 4), ("end", 4), ("P", 5), ("A", 5), ("F", 5, 3), ("G", 5), ("N", 5, 3), ("P", 6), ("yd", 3),
-    ("A", 6), ("G", 6), ("F", 5, 4), ("end", 5), ("P", 3), ("A", 3), ("G", 3), ("P", 7), ("A", 7),
+    ("N", 2, 0), ("F", 3, 0), ("N", 1, 2), ("N", 3, 0), ("F", 0, 3), ("ex", 1), ("N", 0, 3), ("F", 4, 0),
+    ("N", 4, 0), ("F", 1, 3), ("ex", 2), ("F", 2, 1), ("N", 2, 1), ("e2",), ("F", 3, 1), ("N", 1, 3),
+    ("N", 3, 1), ("F", 0, 4), ("end", 0), ("ys", 1, 0), ("ys", 1, 1), ("F", 5, 0), ("N", 5, 0), ("F", 4, 1),
+    ("ex", 3), ("N", 4, 1), ("F", 1, 4), ("end", 1), ("ys", 2, 0), ("ys", 2, 1), ("ys", 3, 0), ("ys", 3, 1),
+    ("yd", 0, 0), ("F", 2, 2), ("N", 2, 2), ("ee",), ("t", 0), ("t", 1), ("F", 3, 2), ("t", 2), ("t", 3),
+    ("N", 3, 2), ("yd", 1, 0), ("F", 5, 1), ("N", 5, 1), ("F", 4, 2), ("N", 4, 2), ("yd", 1, 1), ("F", 2, 3),
+    ("N", 2, 3), ("F", 3, 3), ("P", 0, 1), ("N", 3, 3), ("A", 0, 1), ("F", 5, 2), ("yd", 2, 0), ("G", 0, 1),
+    ("N", 5, 2), ("F", 4, 3), ("N", 4, 3), ("yd", 2, 1), ("F", 2, 4), ("end", 2), ("F", 3, 4), ("end", 3),
+    ("F", 5, 3), ("N", 5, 3), ("P", 2, 4), ("F", 4, 4), ("end", 4), ("yd", 3, 0), ("A", 2, 4), ("G", 2, 4),
+    ("F", 5, 4), ("end", 5), ("P", 5, 6), ("yd", 3, 1), ("A", 5, 6), ("G", 5, 6), ("P", 3, 7), ("A", 3, 7),
 ]
 
 
@@ -148,26 +149,27 @@
             p = wb.at[pl.ds(h0, n), core, row] if kind == "a" else wb.at[h0, core]
             send(p, p, sib_s.at[g], sib_r.at[g], twin)
 
-    def mate_bulk(h):
-        mate_send(7 + h, wb.at[h, core, row])
+    def mate_bulk(h, i):
+        mate_send(6 + 2 * h + i, wb.at[h, core, row, pl.ds(4 * i, 4)])
 
     def mate_b():
         for h in range(4, 8):
             rearrange(h)
-        mate_send(11, wb.at[pl.ds(4, 4), core, row, z])
+        mate_send(14, wb.at[pl.ds(4, 4), core, row, z])
 
     def mate_b_in():
-        arrived(wb.at[pl.ds(4, 4), core, orow, z], wy_s.at[11], wy_r.at[11], mate)
-
-    def mate_done(h):
+        arrived(wb.at[pl.ds(4, 4), core, orow, z], wy_s.at[14], wy_r.at[14], mate)
+
+    def mate_done(h, i):
         if h == 0:
-            for i in range(8):
-                zz = at_z(-i) if i <= 4 else at_z(i - 4)
-                arrived(wb.at[0, core, orow, zz], wy_s.at[i], wy_r.at[i], mate)
+            for j in range(8):
+                zz = at_z(-j) if j <= 4 else at_z(j - 4)
+                arrived(wb.at[0, core, orow, zz], wy_s.at[j], wy_r.at[j], mate)
+            p = wb.at[0, core, orow]
         else:
-            arrived(wb.at[h, core, orow], wy_s.at[7 + h], wy_r.at[7 + h], mate)
-        p = wb.at[h, core, orow]
-        send(p, p, sib_s.at[6 + h], sib_r.at[6 + h], twin)
+            p = wb.at[h, core, orow, pl.ds(4 * i, 4)]
+            arrived(p, wy_s.at[6 + 2 * h + i], wy_r.at[6 + 2 * h + i], mate)
+        send(p, p, sib_s.at[18 + 2 * h + i], sib_r.at[18 + 2 * h + i], twin)
 
     oc = 1 - core
 
@@ -180,8 +182,12 @@
         arrived(p, sib_s.at[g], sib_r.at[g], twin)
 
     def twin_done(h):
-        if h < 4:
-            arrived(wb.at[h, oc, orow], sib_s.at[6 + h], sib_r.at[6 + h], twin)
+        if h == 0:
+            arrived(wb.at[0, oc, orow], sib_s.at[18], sib_r.at[18], twin)
+        elif h < 4:
+            for i in range(2):
+                k = 18 + 2 * h + i
+                arrived(wb.at[h, oc, orow, pl.ds(4 * i, 4)], sib_s.at[k], sib_r.at[k], twin)
         elif h < 7:
             twin_own(h - 2)
         else:
@@ -236,34 +242,37 @@
         b = enc_buf[c // 2, (c % 2) * 8 : (c % 2) * 8 + 8]
         enc_t[:, c * 512 : (c + 1) * 512] = b.reshape(512, TOK).T
 
-    def project(h):
-        w = wb[h].reshape(WIDTH, 2 * HD)
-        kv_v[...] = nn(enc_t[...], w).astype(BF16)
-
-    def attend(h):
-        cols = slice(h * HD, (h + 1) * HD)
-        rows = [slice(i * SEQ, (i + 1) * SEQ) for i in range(TOK // SEQ)]
-        k = [kv_v[r, :HD] for r in rows]
-        v = [kv_v[r, HD:] for r in rows]
-        q = [q_v[r, cols] for r in rows]
-        cg = [cg_v[r, cols] for r in rows]
+    def project(hs):
+        for n, h in enumerate(hs):
+            kv_v[n] = nn(enc_t[...], wb[h].reshape(WIDTH, 2 * HD)).astype(BF16)
+
+    def attend(*hs):
+        at = [
+            (n, slice(i * SEQ, (i + 1) * SEQ), slice(h * HD, (h + 1) * HD))
+            for n, h in enumerate(hs)
+            for i in range(TOK // SEQ)
+        ]
+        k = [kv_v[n, r, :HD] for n, r, _ in at]
+        v = [kv_v[n, r, HD:] for n, r, _ in at]
+        q = [q_v[r, c] for _, r, c in at]
+        cg = [cg_v[r, c] for _, r, c in at]
         s = [nt(a, b) for a, b in zip(k, q)]
         gp = [nt(a, b) for a, b in zip(v, cg)]
         e = [jnp.exp(t - jnp.max(t, axis=0, keepdims=True)) for t in s]
         p = [t * (1.0 / jnp.sum(t, axis=0, keepdims=True)) for t in e]
         pb = [t.astype(BF16) for t in p]
         gs = [(a * (b - jnp.sum(b * a, axis=0, keepdims=True))).astype(BF16) for a, b in zip(p, gp)]
-        for i, r in enumerate(rows):
-            gkv_v[r, :HD] = nn(gs[i], q[i]).astype(BF16)
-            gkv_v[r, HD:] = nn(pb[i], cg[i]).astype(BF16)
-        for i, r in enumerate(rows):
-            ctx_v[r, cols] = tn(pb[i], v[i]).astype(BF16)
-
-    def grad(h):
-        g = gkv_v[...]
+        for i, (n, r, c) in enumerate(at):
+            gkv_v[n, r, :HD] = nn(gs[i], q[i]).astype(BF16)
+            gkv_v[n, r, HD:] = nn(pb[i], cg[i]).astype(BF16)
+        for i, (n, r, c) in enumerate(at):
+            ctx_v[r, c] = tn(pb[i], v[i]).astype(BF16)
+
+    def grad(*hs):
         for c in range(4):
             j, r = c // 2, c % 2
-            t = nt(wb[h, j, r].reshape(512, 2 * HD), g).reshape(NZ, 64, TOK)
+            t = sum(nt(wb[h, j, r].reshape(512, 2 * HD), gkv_v[n]) for n, h in enumerate(hs))
+            t = t.reshape(NZ, 64, TOK)
             acc[j, r] = t if first[0] else acc[j, r] + t
         first[0] = False
 
@@ -284,12 +293,13 @@
 
     owned = set()
 
-    def project_step(h):
-        if h < 4 and h // 2 not in owned:
-            owned.add(h // 2)
-            twin_own(h // 2)
-        twin_done(h)
-        project(h)
+    def project_step(*hs):
+        for h in hs:
+            if h < 4 and h // 2 not in owned:
+                owned.add(h // 2)
+                twin_own(h // 2)
+            twin_done(h)
+        project(hs)
 
     steps = {
         "e0": own_start, "e1": enc_1, "e2": enc_2, "ex": enc_hop, "ee": enc_all, "t": transpose,
@@ -301,15 +311,16 @@
 
     out_ctx = pltpu.make_async_copy(ctx_v, ctx_ref, loc.at[4])
     out_ctx.start()
-    g7 = gkv_v[...]
+    final = [at for name, *at in ORDER if name == "P"][-1]
+    g_last = [gkv_v[n] for n in range(len(final))]
     order = (yo, yp, ym, y)
 
     def blocks(ref, j, xx):
         return ref.at[j, xx // 2, pl.ds((xx % 2) * 4, 4)]
 
     def last(j, xx):
-        w = blocks(wb.at[7], j, xx)[...].reshape(TOK, 2 * HD)
-        return blocks(acc, j, xx)[...] + nt(w, g7).reshape(4, 64, TOK)
+        t = sum(nt(blocks(wb.at[h], j, xx)[...].reshape(TOK, 2 * HD), g) for h, g in zip(final, g_last))
+        return blocks(acc, j, xx)[...] + t.reshape(4, 64, TOK)
 
     def one(j, xx, yy):
         return acc.at[j, xx // 2, (xx % 2) * 4 + yy]
@@ -357,31 +368,60 @@
         t0 = one(0, x, order[r])[...] + gx_in(3, r)
         return t0 + gx_in(4, r), t1 + gx_in(5, r)
 
-    def gy(m, v):
-        ys[m] = v.astype(BF16)
-        send(ys.at[m], yr.at[m], gy_s.at[m], gy_r.at[m], y_up if m % 2 == 0 else y_dn)
-
-    def gy_in(m):
-        arrived(yr.at[m], gy_s.at[m], gy_r.at[m], y_dn if m % 2 == 0 else y_up)
-        return yr[m].astype(F32)
+    def gy(m, i, v):
+        half = pl.ds(32 * i, 32)
+        ys[m, half] = v.astype(BF16)
+        dev = y_up if m % 2 == 0 else y_dn
+        send(ys.at[m, half], yr.at[m, half], gy_s.at[m, i], gy_r.at[m, i], dev)
+
+    def gy_in(m, i):
+        half = pl.ds(32 * i, 32)
+        arrived(yr.at[m, half], gy_s.at[m, i], gy_r.at[m, i], y_dn if m % 2 == 0 else y_up)
+        return yr[m, half].astype(F32)
+
+    def part(v, i):
+        return v[32 * i : 32 * i + 32]
 
     s0, s1 = total(0)
-    gy(0, s0)
-    gy(1, s1)
+    for i in range(2):
+        gy(0, i, part(s0, i))
+        gy(1, i, part(s1, i))
     relay(3)
     u0, u1 = total(1)
-    gy(2, u1)
+    for i in range(2):
+        gy(2, i, part(u1, i))
     d0, d1 = total(2)
-    gy(3, d0)
-    gy(4, u0 + gy_in(0))
-    gy(5, d1 + gy_in(1))
+    for i in range(2):
+        gy(3, i, part(d0, i))
+    while started:
+        started.pop(0).wait_send()
+    for i in range(2):
+        gy(4, i, part(u0, i) + gy_in(0, i))
+        gy(5, i, part(d1, i) + gy_in(1, i))
     o0, o1 = total(3)
-    ge_ref[0] = (o0 + gy_in(3) + gy_in(4)).astype(BF16)
-    ge_ref[1] = (o1 + gy_in(2) + gy_in(5)).astype(BF16)
+    for i in range(2):
+        half = slice(32 * i, 32 * i + 32)
+        ge_ref[0, half] = (part(o0, i) + gy_in(3, i) + gy_in(4, i)).astype(BF16)
+        ge_ref[1, half] = (part(o1, i) + gy_in(2, i) + gy_in(5, i)).astype(BF16)
 
     for c in started:
         c.wait_send()
     out_ctx.wait()
+
+
+def hand_on(ctx_ref, ge_ref, ctx_out, ge_out, ctx_v, ge_v, sem_in, sem_out):
+    rows = TOK // PARTS
+    parts = [tuple(r.at[pl.ds(i * rows, rows)] for r in (ctx_ref, ctx_v, ctx_out)) for i in range(PARTS)]
+    parts.append((ge_ref, ge_v, ge_out))
+    there = [pltpu.make_async_copy(s, v, sem_in.at[i]) for i, (s, v, _) in enumerate(parts)]
+    on = [pltpu.make_async_copy(v, d, sem_out.at[i]) for i, (_, v, d) in enumerate(parts)]
+    for c in there:
+        c.start()
+    for a, b in zip(there, on):
+        a.wait()
+        b.start()
+    for c in on:
+        c.wait()
 
 
 def local(encoder_out, key_value_weight, queries, context_gradient):
@@ -405,8 +445,8 @@
             pltpu.VMEM((TOK, HEADS * HD), BF16),
             pltpu.VMEM((TOK, HEADS * HD), BF16),
             pltpu.VMEM((TOK, HEADS * HD), BF16),
-            pltpu.VMEM((TOK, 2 * HD), BF16),
-            pltpu.VMEM((TOK, 2 * HD), BF16),
+            pltpu.VMEM((2, TOK, 2 * HD), BF16),
+            pltpu.VMEM((2, TOK, 2 * HD), BF16),
             pltpu.VMEM((6, 4, 64, TOK), BF16),
             pltpu.VMEM((6, 4, 64, TOK), BF16),
             pltpu.VMEM((6, 64, TOK), BF16),
@@ -414,19 +454,19 @@
             dma((5,)),
             dma((6, 7)),
             dma((6, 7)),
-            dma((12,)),
-            dma((12,)),
-            dma((18,)),
-            dma((18,)),
+            dma((15,)),
+            dma((15,)),
+            dma((26,)),
+            dma((26,)),
             dma((20,)),
             dma((20,)),
             dma((6, 4)),
             dma((6, 4)),
-            dma((6,)),
-            dma((6,)),
+            dma((6, 2)),
+            dma((6, 2)),
         ],
         compiler_params=pltpu.CompilerParams(
-            collective_id=0, has_side_effects=True, vmem_limit_bytes=LIMIT * 1024 * 1024
+            collective_id=0, has_side_effects=True, vmem_limit_bytes=LIMIT * 1024
         ),
     )(
         encoder_out.reshape(2, 64, TOK),
@@ -434,6 +474,22 @@
         queries[0],
         context_gradient[0],
     )
+    ctx, ge = pl.pallas_call(
+        hand_on,
+        out_shape=(
+            jax.ShapeDtypeStruct((TOK, HEADS * HD), BF16),
+            jax.ShapeDtypeStruct((2, 64, TOK), BF16),
+        ),
+        in_specs=[any_space] * 2,
+        out_specs=(any_space, any_space),
+        scratch_shapes=[
+            pltpu.VMEM((TOK, HEADS * HD), BF16),
+            pltpu.VMEM((2, 64, TOK), BF16),
+            dma((PARTS + 1,)),
+            dma((PARTS + 1,)),
+        ],
+        compiler_params=pltpu.CompilerParams(vmem_limit_bytes=LIMIT * 1024),
+    )(ctx, ge)
     return ctx[None], ge.reshape(2 * 64, TOK)
 
 

time: 76.5 us -> 73.2 us (0.957)
  local copies, waits for them, and re-layouts: 2.53 us -> 0 us
    pallas_call x1, Pallas kernels: 72 us -> 69.4 us  [local(): pl.pallas_call(kernel, out_shape=(jax.ShapeDtypeStruct((TOK, HEADS * HD),...]
    unnamed x4 -> x0, local copies, waits for them, and re-layouts: 2.53 us -> none
    pallas_call x0 -> x1, Pallas kernels: none -> 1.85 us  [local(): pl.pallas_call(hand_on, out_shape=(jax.ShapeDtypeStruct((TOK, HEADS * HD)...]
where the time goes in v3:
time: 73.2 us; the launch traced here: 71.9 us
  Pallas kernels  71.3 us (97%)
    pallas_call x1, Pallas kernels, local(): pl.pallas_call(kernel, out_shape=(jax.ShapeDtypeStruct((TOK, HEADS * HD),...  69.4 us
    pallas_call x1, Pallas kernels, local(): pl.pallas_call(hand_on, out_shape=(jax.ShapeDtypeStruct((TOK, HEADS * HD)...  1.85 us

profile of v3, /device:TPU:1, one launch (start us, length us, event | category | flops | bytes accessed | tf_op | source)
XLA Modules:
  0.0 71.9 jit_solution(3705366834790622771)
XLA Ops:
  0.6 69.4 %shard_map.59 = (bf16[256,1024]{1,0:T(8,128)(2,1)}, bf16[2,64,256]{2,1,0:T(8,128)(2,1)}) custom-call(bf16[2,64,256]{2,1,0:T(8,128)(2,1)} %bitcast.9, bf16[64,2048]{1,0:T(8,128)(2,1)} %bitcast.8, bf16[256,1024]{1,0:T(8,128)(2,1)} %bitcast.6, bf16[256,1024]{1,0:T(8,128)(2,1)} %bitcast.7), custom_call_target="tpu_custom_call" | custom-call | tf_op jit(solution)/shard_map/pallas_call | solution.py:431
  70.1 1.9 %shard_map.60 = (bf16[256,1024]{1,0:T(8,128)(2,1)}, bf16[2,64,256]{2,1,0:T(8,128)(2,1)}) custom-call(bf16[256,1024]{1,0:T(8,128)(2,1)} %get-tuple-element.6.ctx_ref, bf16[2,64,256]{2,1,0:T(8,128)(2,1)} %get-tuple-element.7.ge_ref), custom_call_target="tpu_custom_call" | custom-call | tf_op jit(solution)/shard_map/pallas_call | solution.py:477

commit v4 on v3

--- a/solution.py
+++ b/solution.py
@@ -12,6 +12,7 @@
 TOK = 256
 WIDTH = 2048
 NZ = 8
+KEEP = 16
 PARTS = 4
 LIMIT = 63488
 F32 = jnp.float32
@@ -20,16 +21,16 @@
 ORDER = [
     ("e0",), ("yb",), ("F", 0, 0), ("N", 0, 0), ("F", 1, 0), ("N", 1, 0), ("F", 0, 1), ("ex", 0), ("N", 0, 1),
     ("F", 1, 1), ("N", 1, 1), ("e1",), ("F", 0, 2), ("N", 0, 2), ("F", 1, 2), ("ybw",), ("F", 2, 0),
-    ("N", 2, 0), ("F", 3, 0), ("N", 1, 2), ("N", 3, 0), ("F", 0, 3), ("ex", 1), ("N", 0, 3), ("F", 4, 0),
-    ("N", 4, 0), ("F", 1, 3), ("ex", 2), ("F", 2, 1), ("N", 2, 1), ("e2",), ("F", 3, 1), ("N", 1, 3),
-    ("N", 3, 1), ("F", 0, 4), ("end", 0), ("ys", 1, 0), ("ys", 1, 1), ("F", 5, 0), ("N", 5, 0), ("F", 4, 1),
-    ("ex", 3), ("N", 4, 1), ("F", 1, 4), ("end", 1), ("ys", 2, 0), ("ys", 2, 1), ("ys", 3, 0), ("ys", 3, 1),
-    ("yd", 0, 0), ("F", 2, 2), ("N", 2, 2), ("ee",), ("t", 0), ("t", 1), ("F", 3, 2), ("t", 2), ("t", 3),
-    ("N", 3, 2), ("yd", 1, 0), ("F", 5, 1), ("N", 5, 1), ("F", 4, 2), ("N", 4, 2), ("yd", 1, 1), ("F", 2, 3),
-    ("N", 2, 3), ("F", 3, 3), ("P", 0, 1), ("N", 3, 3), ("A", 0, 1), ("F", 5, 2), ("yd", 2, 0), ("G", 0, 1),
-    ("N", 5, 2), ("F", 4, 3), ("N", 4, 3), ("yd", 2, 1), ("F", 2, 4), ("end", 2), ("F", 3, 4), ("end", 3),
-    ("F", 5, 3), ("N", 5, 3), ("P", 2, 4), ("F", 4, 4), ("end", 4), ("yd", 3, 0), ("A", 2, 4), ("G", 2, 4),
-    ("F", 5, 4), ("end", 5), ("P", 5, 6), ("yd", 3, 1), ("A", 5, 6), ("G", 5, 6), ("P", 3, 7), ("A", 3, 7),
+    ("N", 2, 0), ("F", 3, 0), ("N", 3, 0), ("N", 1, 2), ("ex", 1), ("F", 0, 3), ("N", 0, 3), ("F", 4, 0),
+    ("N", 4, 0), ("ex", 2), ("F", 1, 3), ("F", 2, 1), ("N", 2, 1), ("F", 3, 1), ("N", 3, 1), ("e2",),
+    ("N", 1, 3), ("F", 0, 4), ("F", 5, 0), ("N", 5, 0), ("end", 0), ("F", 4, 1), ("N", 4, 1), ("F", 1, 4),
+    ("end", 1), ("ys", 2, 0), ("ys", 2, 1), ("ys", 3, 0), ("ex", 3), ("F", 2, 2), ("ys", 3, 1), ("N", 2, 2),
+    ("F", 3, 2), ("N", 3, 2), ("yd", 0, 0), ("F", 5, 1), ("ee",), ("t", 0), ("t", 1), ("N", 5, 1), ("t", 2),
+    ("t", 3), ("F", 4, 2), ("P", 0, 1), ("N", 4, 2), ("yd", 2, 0), ("F", 2, 3), ("A", 0, 1), ("N", 2, 3),
+    ("G", 0, 1), ("F", 3, 3), ("N", 3, 3), ("yd", 2, 1), ("F", 5, 2), ("N", 5, 2), ("F", 4, 3), ("N", 4, 3),
+    ("yd", 3, 0), ("F", 2, 4), ("end", 2), ("F", 3, 4), ("end", 3), ("F", 5, 3), ("N", 5, 3), ("P", 2, 4),
+    ("F", 4, 4), ("end", 4), ("yd", 3, 1), ("A", 2, 4), ("G", 2, 4), ("F", 5, 4), ("end", 5), ("P", 5, 6),
+    ("A", 5, 6), ("G", 5, 6), ("P", 3, 7), ("A", 3, 7),
 ]
 
 
@@ -82,6 +83,10 @@
         c.start()
         started.append(c)
 
+    def sent(keep):
+        while len(started) > keep:
+            started.pop(0).wait_send()
+
     def arrived(dst, ss, rs, dev):
         pltpu.make_async_remote_copy(
             src_ref=dst, dst_ref=dst, send_sem=ss, recv_sem=rs, device_id=dev, device_id_type=MESH
@@ -118,7 +123,7 @@
 
     def spread(g, k, zz):
         if g == 0:
-            mate_send(k, wb.at[0, core, row, zz])
+            mate_send(k, piece(0, zz))
         if g == 5:
             p = piece(g, zz)
             send(p, p, sib_s.at[10 + k], sib_r.at[10 + k], twin)
@@ -164,8 +169,8 @@
         if h == 0:
             for j in range(8):
                 zz = at_z(-j) if j <= 4 else at_z(j - 4)
-                arrived(wb.at[0, core, orow, zz], wy_s.at[j], wy_r.at[j], mate)
-            p = wb.at[0, core, orow]
+                arrived(wb.at[pl.ds(0, 2), core, orow, zz], wy_s.at[j], wy_r.at[j], mate)
+            p = wb.at[pl.ds(0, 2), core, orow]
         else:
             p = wb.at[h, core, orow, pl.ds(4 * i, 4)]
             arrived(p, wy_s.at[6 + 2 * h + i], wy_r.at[6 + 2 * h + i], mate)
@@ -182,8 +187,10 @@
         arrived(p, sib_s.at[g], sib_r.at[g], twin)
 
     def twin_done(h):
-        if h == 0:
-            arrived(wb.at[0, oc, orow], sib_s.at[18], sib_r.at[18], twin)
+        if h < 2:
+            if "pair" not in owned:
+                owned.add("pair")
+                arrived(wb.at[pl.ds(0, 2), oc, orow], sib_s.at[18], sib_r.at[18], twin)
         elif h < 4:
             for i in range(2):
                 k = 18 + 2 * h + i
@@ -307,6 +314,8 @@
         "ys": mate_bulk, "yd": mate_done, "P": project_step, "A": attend, "G": grad,
     }
     for name, *at in ORDER:
+        if name == "P":
+            sent(KEEP)
         steps[name](*at)
 
     out_ctx = pltpu.make_async_copy(ctx_v, ctx_ref, loc.at[4])
@@ -351,6 +360,7 @@
     xs[3] = last(0, xm).astype(BF16)
     pair(2, 0)
     pair(0, 2)
+    sent(8)
     blocks(acc, 0, xp)[...] = last(0, xp)
     blocks(acc, 1, xm)[...] = last(1, xm)
     relay(0)
@@ -393,8 +403,6 @@
     d0, d1 = total(2)
     for i in range(2):
         gy(3, i, part(d0, i))
-    while started:
-        started.pop(0).wait_send()
     for i in range(2):
         gy(4, i, part(u0, i) + gy_in(0, i))
         gy(5, i, part(d1, i) + gy_in(1, i))
@@ -404,8 +412,7 @@
         ge_ref[0, half] = (part(o0, i) + gy_in(3, i) + gy_in(4, i)).astype(BF16)
         ge_ref[1, half] = (part(o1, i) + gy_in(2, i) + gy_in(5, i)).astype(BF16)
 
-    for c in started:
-        c.wait_send()
+    sent(0)
     out_ctx.wait()
 
 

time: 73.2 us -> 71.8 us (0.981); the launches traced: 71.9 us -> 71.4 us
  no operation moved by 1% of the time
where the time goes in v4:
time: 71.8 us; the launch traced here: 71.4 us
  Pallas kernels  70.8 us (99%)
    pallas_call x1, Pallas kernels, local(): pl.pallas_call(kernel, out_shape=(jax.ShapeDtypeStruct((TOK, HEADS * HD),...  68.9 us
    pallas_call x1, Pallas kernels, local(): pl.pallas_call(hand_on, out_shape=(jax.ShapeDtypeStruct((TOK, HEADS * HD)...  1.85 us

profile of v4, /device:TPU:1, one launch (start us, length us, event | category | flops | bytes accessed | tf_op | source)
XLA Modules:
  0.0 71.4 jit_solution(15946571676216216567)
XLA Ops:
  0.6 68.9 %shard_map.59 = (bf16[256,1024]{1,0:T(8,128)(2,1)}, bf16[2,64,256]{2,1,0:T(8,128)(2,1)}) custom-call(bf16[2,64,256]{2,1,0:T(8,128)(2,1)} %bitcast.9, bf16[64,2048]{1,0:T(8,128)(2,1)} %bitcast.8, bf16[256,1024]{1,0:T(8,128)(2,1)} %bitcast.6, bf16[256,1024]{1,0:T(8,128)(2,1)} %bitcast.7), custom_call_target="tpu_custom_call" | custom-call | tf_op jit(solution)/shard_map/pallas_call | solution.py:438
  69.5 1.9 %shard_map.60 = (bf16[256,1024]{1,0:T(8,128)(2,1)}, bf16[2,64,256]{2,1,0:T(8,128)(2,1)}) custom-call(bf16[256,1024]{1,0:T(8,128)(2,1)} %get-tuple-element.6.ctx_ref, bf16[2,64,256]{2,1,0:T(8,128)(2,1)} %get-tuple-element.7.ge_ref), custom_call_target="tpu_custom_call" | custom-call | tf_op jit(solution)/shard_map/pallas_call | solution.py:484

commit v5 on v4

--- a/solution.py
+++ b/solution.py
@@ -355,22 +355,22 @@
     xs[0] = last(0, xo).astype(BF16)
     xs[1] = last(1, xo).astype(BF16)
     pair(0, 0)
-    pair(0, 1)
     xs[2] = last(1, xp).astype(BF16)
     xs[3] = last(0, xm).astype(BF16)
     pair(2, 0)
+    pair(0, 1)
     pair(0, 2)
     sent(8)
     blocks(acc, 0, xp)[...] = last(0, xp)
     blocks(acc, 1, xm)[...] = last(1, xm)
     relay(0)
-    pair(0, 3)
     pair(2, 1)
     blocks(acc, 0, x)[...] = last(0, x)
     blocks(acc, 1, x)[...] = last(1, x)
     relay(1)
     pair(2, 2)
     relay(2)
+    pair(0, 3)
     pair(2, 3)
 
     def total(r):
@@ -396,13 +396,13 @@
     for i in range(2):
         gy(0, i, part(s0, i))
         gy(1, i, part(s1, i))
-    relay(3)
     u0, u1 = total(1)
     for i in range(2):
         gy(2, i, part(u1, i))
     d0, d1 = total(2)
     for i in range(2):
         gy(3, i, part(d0, i))
+    relay(3)
     for i in range(2):
         gy(4, i, part(u0, i) + gy_in(0, i))
         gy(5, i, part(d1, i) + gy_in(1, i))

time: 71.8 us -> 71.5 us (level)
  no operation moved by 1% of the time
where the time goes in v5:
time: 71.5 us; the launch traced here: 70.8 us
  Pallas kernels  70.2 us (98%)
    pallas_call x1, Pallas kernels, local(): pl.pallas_call(kernel, out_shape=(jax.ShapeDtypeStruct((TOK, HEADS * HD),...  68.3 us
    pallas_call x1, Pallas kernels, local(): pl.pallas_call(hand_on, out_shape=(jax.ShapeDtypeStruct((TOK, HEADS * HD)...  1.85 us

profile of v5, /device:TPU:1, one launch (start us, length us, event | category | flops | bytes accessed | tf_op | source)
XLA Modules:
  0.0 70.8 jit_solution(9472753639298924144)
XLA Ops:
  0.6 68.3 %shard_map.59 = (bf16[256,1024]{1,0:T(8,128)(2,1)}, bf16[2,64,256]{2,1,0:T(8,128)(2,1)}) custom-call(bf16[2,64,256]{2,1,0:T(8,128)(2,1)} %bitcast.9, bf16[64,2048]{1,0:T(8,128)(2,1)} %bitcast.8, bf16[256,1024]{1,0:T(8,128)(2,1)} %bitcast.6, bf16[256,1024]{1,0:T(8,128)(2,1)} %bitcast.7), custom_call_target="tpu_custom_call" | custom-call | tf_op jit(solution)/shard_map/pallas_call | solution.py:438
  69.0 1.9 %shard_map.60 = (bf16[256,1024]{1,0:T(8,128)(2,1)}, bf16[2,64,256]{2,1,0:T(8,128)(2,1)}) custom-call(bf16[256,1024]{1,0:T(8,128)(2,1)} %get-tuple-element.6.ctx_ref, bf16[2,64,256]{2,1,0:T(8,128)(2,1)} %get-tuple-element.7.ge_ref), custom_call_target="tpu_custom_call" | custom-call | tf_op jit(solution)/shard_map/pallas_call | solution.py:484

commit v6 on v5

--- a/solution.py
+++ b/solution.py
@@ -13,7 +13,7 @@
 WIDTH = 2048
 NZ = 8
 KEEP = 16
-PARTS = 4
+PARTS = 2
 LIMIT = 63488
 F32 = jnp.float32
 BF16 = jnp.bfloat16
@@ -21,16 +21,16 @@
 ORDER = [
     ("e0",), ("yb",), ("F", 0, 0), ("N", 0, 0), ("F", 1, 0), ("N", 1, 0), ("F", 0, 1), ("ex", 0), ("N", 0, 1),
     ("F", 1, 1), ("N", 1, 1), ("e1",), ("F", 0, 2), ("N", 0, 2), ("F", 1, 2), ("ybw",), ("F", 2, 0),
-    ("N", 2, 0), ("F", 3, 0), ("N", 3, 0), ("N", 1, 2), ("ex", 1), ("F", 0, 3), ("N", 0, 3), ("F", 4, 0),
-    ("N", 4, 0), ("ex", 2), ("F", 1, 3), ("F", 2, 1), ("N", 2, 1), ("F", 3, 1), ("N", 3, 1), ("e2",),
-    ("N", 1, 3), ("F", 0, 4), ("F", 5, 0), ("N", 5, 0), ("end", 0), ("F", 4, 1), ("N", 4, 1), ("F", 1, 4),
+    ("N", 2, 0), ("F", 3, 0), ("N", 3, 0), ("F", 4, 0), ("N", 1, 2), ("N", 4, 0), ("ex", 1), ("F", 0, 3),
+    ("N", 0, 3), ("ex", 2), ("F", 1, 3), ("F", 2, 1), ("N", 2, 1), ("F", 3, 1), ("N", 3, 1), ("e2",),
+    ("F", 4, 1), ("N", 1, 3), ("F", 5, 0), ("N", 5, 0), ("N", 4, 1), ("F", 0, 4), ("end", 0), ("F", 1, 4),
     ("end", 1), ("ys", 2, 0), ("ys", 2, 1), ("ys", 3, 0), ("ex", 3), ("F", 2, 2), ("ys", 3, 1), ("N", 2, 2),
-    ("F", 3, 2), ("N", 3, 2), ("yd", 0, 0), ("F", 5, 1), ("ee",), ("t", 0), ("t", 1), ("N", 5, 1), ("t", 2),
-    ("t", 3), ("F", 4, 2), ("P", 0, 1), ("N", 4, 2), ("yd", 2, 0), ("F", 2, 3), ("A", 0, 1), ("N", 2, 3),
-    ("G", 0, 1), ("F", 3, 3), ("N", 3, 3), ("yd", 2, 1), ("F", 5, 2), ("N", 5, 2), ("F", 4, 3), ("N", 4, 3),
-    ("yd", 3, 0), ("F", 2, 4), ("end", 2), ("F", 3, 4), ("end", 3), ("F", 5, 3), ("N", 5, 3), ("P", 2, 4),
-    ("F", 4, 4), ("end", 4), ("yd", 3, 1), ("A", 2, 4), ("G", 2, 4), ("F", 5, 4), ("end", 5), ("P", 5, 6),
-    ("A", 5, 6), ("G", 5, 6), ("P", 3, 7), ("A", 3, 7),
+    ("F", 3, 2), ("N", 3, 2), ("yd", 0, 0), ("F", 4, 2), ("ee",), ("t", 0), ("t", 1), ("F", 5, 1), ("t", 2),
+    ("t", 3), ("N", 5, 1), ("P", 0, 1), ("N", 4, 2), ("yd", 2, 0), ("F", 2, 3), ("A", 0, 1), ("N", 2, 3),
+    ("G", 0, 1), ("F", 3, 3), ("N", 3, 3), ("yd", 2, 1), ("F", 4, 3), ("F", 5, 2), ("N", 5, 2), ("N", 4, 3),
+    ("yd", 3, 0), ("F", 2, 4), ("end", 2), ("F", 3, 4), ("end", 3), ("F", 4, 4), ("end", 4), ("F", 5, 3),
+    ("P", 2, 4), ("N", 5, 3), ("yd", 3, 1), ("A", 2, 4), ("G", 2, 4), ("P", 5, 6), ("A", 5, 6), ("F", 5, 4),
+    ("end", 5), ("G", 5, 6), ("P", 3, 7), ("A", 3, 7),
 ]
 
 

time: 71.5 us -> 71.2 us (level)
  no operation moved by 1% of the time
where the time goes in v6:
time: 71.2 us; the launch traced here: 70.3 us
  Pallas kernels  69.7 us (98%)
    pallas_call x1, Pallas kernels, local(): pl.pallas_call(kernel, out_shape=(jax.ShapeDtypeStruct((TOK, HEADS * HD),...  67.9 us
    pallas_call x1, Pallas kernels, local(): pl.pallas_call(hand_on, out_shape=(jax.ShapeDtypeStruct((TOK, HEADS * HD)...  1.8 us

profile of v6, /device:TPU:1, one launch (start us, length us, event | category | flops | bytes accessed | tf_op | source)
XLA Modules:
  0.0 70.3 jit_solution(341998062690572232)
XLA Ops:
  0.6 67.9 %shard_map.59 = (bf16[256,1024]{1,0:T(8,128)(2,1)}, bf16[2,64,256]{2,1,0:T(8,128)(2,1)}) custom-call(bf16[2,64,256]{2,1,0:T(8,128)(2,1)} %bitcast.9, bf16[64,2048]{1,0:T(8,128)(2,1)} %bitcast.8, bf16[256,1024]{1,0:T(8,128)(2,1)} %bitcast.6, bf16[256,1024]{1,0:T(8,128)(2,1)} %bitcast.7), custom_call_target="tpu_custom_call" | custom-call | tf_op jit(solution)/shard_map/pallas_call | solution.py:438
  68.5 1.8 %shard_map.60 = (bf16[256,1024]{1,0:T(8,128)(2,1)}, bf16[2,64,256]{2,1,0:T(8,128)(2,1)}) custom-call(bf16[256,1024]{1,0:T(8,128)(2,1)} %get-tuple-element.6.ctx_ref, bf16[2,64,256]{2,1,0:T(8,128)(2,1)} %get-tuple-element.7.ge_ref), custom_call_target="tpu_custom_call" | custom-call | tf_op jit(solution)/shard_map/pallas_call | solution.py:484
